TPU v7x, 32 devices: a whole 2x2x4 slice. The times are simulated.
32 devices in a mesh: scen: 8 (over z, y), tile: 4 (over x, core).
Axes of the slice: x: 2, y: 2, z: 4, core: 2. Of those that a mesh axis runs over, the one named last changes fastest.
Arguments:
- factor_inv: bfloat16 [64, 768, 768], P('scen'), may hold values from -0.21875 to 0.21875
- pattern: int32 [64, 6, 6], P('scen'), may hold values 0 or 1
- border: bfloat16 [64, 768, 512], P('scen', None, 'tile'), may hold values from -0.59765625 to 0.59765625
- row_scale: float32 [64, 768], P('scen'), may hold values from 0.25 to 4
- link_ids: int32 [64, 4], P('scen'), may hold values from 0 to 63, as said below
- first_diag: float32 [8192], replicated, may hold values from 10 to 100
Outputs:
- schur: float32 [8192, 8192], P('tile', 'scen')
Inputs may be any that keep to these rules, and one draw needn't show every extreme that they name: link_ids[s, j] lies in group j, that is among blocks j * 16 to (j + 1) * 16 - 1. For each aligned block of 8 scenarios and each group, at most 6 of those scenarios link to one run of 8 blocks starting at a multiple of 8, and one such run has exactly 6.
All inputs are finite; a program needn't handle non-finite values. No bound on the sum of `pattern` on one device may be relied on, other than what follows from the above.
Results may differ from a plain program's by a relative error of at most 0.003.
Values may be sent and summed in bfloat16 or wider, within the bound.
A program may use at most 128 MiB of HBM per device.

v0:
```python
import jax
import jax.numpy as jnp
from jax import lax
from jax.sharding import PartitionSpec as P


def on_device(factor_inv, pattern, border, row_scale, link_ids, first_diag):
    local_scen, scen_rows, _ = factor_inv.shape
    block_count = pattern.shape[1]
    block_size = border.shape[2]
    order_size = first_diag.shape[0]
    tile_count = lax.axis_size("tile")
    owner_count = lax.axis_size("scen")
    tile_id = lax.axis_index("tile")
    owner_id = lax.axis_index("scen")
    group_blocks = order_size // (tile_count * block_size)
    owner_blocks = order_size // (owner_count * block_size)
    owners_group = owner_count // tile_count
    capacity = local_scen // owners_group + local_scen // (2 * owners_group)
    index_blocks = jnp.arange(block_count)
    diagonal_mask = index_blocks[:, None] == index_blocks[None, :]
    below_diag = (index_blocks[:, None] > index_blocks[None, :]).astype(jnp.int32)
    effective = jnp.where(diagonal_mask[None], 1, pattern * below_diag[None])
    shaped = factor_inv.reshape(local_scen, block_count, block_size, block_count, block_size)
    masked = (shaped * effective[:, :, None, :, None].astype(jnp.bfloat16)).reshape(
        local_scen, scen_rows, scen_rows
    )
    solved_own = jnp.einsum(
        "snm,smc->snc", masked, border, preferred_element_type=jnp.float32
    ).astype(jnp.bfloat16)
    scaled = (row_scale[:, :, None] * solved_own.astype(jnp.float32)).astype(jnp.bfloat16)
    row_blocks = jnp.einsum(
        "snr,snc->src",
        scaled,
        lax.all_gather(solved_own, "tile", axis=2, tiled=True),
        preferred_element_type=jnp.float32,
    )
    blocks_out = jnp.transpose(
        row_blocks.reshape(local_scen, block_size, tile_count, block_size), (0, 2, 1, 3)
    )
    destination = link_ids // owner_blocks
    same_owner = destination[:, None, :] == destination[None, :, :]
    scen_index = jnp.arange(local_scen)
    earlier = (scen_index[None, :] < scen_index[:, None])[:, :, None]
    slot_rank = jnp.sum((same_owner & earlier).astype(jnp.int32), axis=1)
    own_links = lax.dynamic_slice_in_dim(link_ids, tile_id, 1, 1)[:, 0]
    row_local = own_links - tile_id * group_blocks
    target = row_local[:, None] * owner_blocks + link_ids % owner_blocks
    bin_count = group_blocks * owner_blocks
    send_blocks = jnp.zeros((owner_count, capacity, block_size, block_size), jnp.float32)
    send_blocks = send_blocks.at[destination, slot_rank].set(blocks_out)
    send_targets = jnp.full((owner_count, capacity), bin_count, jnp.int32)
    send_targets = send_targets.at[destination, slot_rank].set(target)
    received, received_targets = (
        lax.all_to_all(
            send_blocks.astype(jnp.bfloat16), "scen", split_axis=0, concat_axis=0, tiled=True
        ).astype(send_blocks.dtype),
        lax.all_to_all(send_targets, "scen", split_axis=0, concat_axis=0, tiled=True),
    )
    target_bins = jnp.zeros((bin_count + 1, block_size, block_size), jnp.float32)
    target_bins = target_bins.at[received_targets.reshape(-1)].add(
        received.reshape(-1, block_size, block_size)
    )
    tile_rows = group_blocks * block_size
    tile_cols = owner_blocks * block_size
    tile_out = jnp.transpose(
        target_bins[:bin_count].reshape(group_blocks, owner_blocks, block_size, block_size),
        (0, 2, 1, 3),
    ).reshape(tile_rows, tile_cols)
    row_start = tile_id * tile_rows
    col_start = owner_id * tile_cols
    global_rows = row_start + jnp.arange(tile_rows)
    global_cols = col_start + jnp.arange(tile_cols)
    diag_values = lax.dynamic_slice_in_dim(first_diag, row_start, tile_rows)
    on_diagonal = global_rows[:, None] == global_cols[None, :]
    return tile_out + jnp.where(on_diagonal, diag_values[:, None], 0.0)


def solution(mesh):
    in_specs = (
        P("scen", None, None),
        P("scen", None, None),
        P("scen", None, "tile"),
        P("scen", None),
        P("scen", None),
        P(),
    )
    out_specs = P("tile", "scen")
    return jax.shard_map(
        on_device, mesh=mesh, in_specs=in_specs, out_specs=out_specs, check_vma=False
    )
```

profile of v0, /device:TPU:2, one launch (start us, length us, event | category | flops | bytes accessed | tf_op | source)
XLA Modules:
  0.0 191.1 jit_solution(647858114984788605)
XLA Ops:
  6.5 0.0 copy-start
  6.5 0.0 all-gather.2.cloned.1.call-start
  6.5 0.9 select_convert_fusion
  7.4 6.2 %mul.46 = bf16[8,6,128,6,128]{4,3,2,1,0:T(8,128)(2,1)} broadcast(bf16[8,6,6]{2,1,0:T(8,128)(2,1)S(1)} %copy.37), dimensions={0,1,3} | broadcast | bytes 9437760 | tf_op jit(solution)/shard_map/mul | solution.py:25
  13.7 20.4 %mul.47 = bf16[8,768,768]{2,1,0:T(8,128)(2,1)} reshape(bf16[8,6,128,6,128]{4,3,2,1,0:T(8,128)(2,1)} %mul.46) | data formatting | bytes 18874368 | tf_op jit(solution)/shard_map/mul | solution.py:25
  34.0 0.0 copy-done
  34.0 0.0 copy-start.4
  34.0 10.1 %fusion.2 = bf16[8,768,128]{2,1,0:T(8,128)(2,1)} fusion(bf16[8,768,128]{2,1,0:T(8,128)(2,1)S(1)} %copy-done, bf16[8,768,768]{2,1,0:T(8,128)(2,1)} %param.6, bf16[8,768,768]{2,1,0:T(8,128)(2,1)} %mul.47), kind=kOutput, calls=%fused_computation.8 | convolution fusion | flops 1213464576 | bytes 22020096 | tf_op jit(solution)/shard_map/snm,smc->snc/dot_general | solution.py:28
  44.1 0.0 all-gather.2.cloned.1.call-update
  44.2 0.0 copy-done.4
  44.2 0.2 convert_reduce_fusion
  44.5 0.1 copy.34
  44.5 0.1 reshape.125
  44.6 0.1 copy.35
  44.7 0.1 reshape.127
  44.8 0.6 broadcast_in_dim.29
  45.4 0.0 copy-start.2
  45.4 0.0 copy-start.3
  45.4 5.3 %scatter_fusion = s32[8,6]{1,0:T(8,128)} fusion(s32[8,6]{1,0:T(8,128)} %broadcast_in_dim.29, s32[32]{0:T(128)S(1)} %reshape.125, s32[32]{0:T(128)S(1)} %reshape.127), kind=kCustom, calls=%fused_computation | custom fusion | bytes 640 | tf_op jit(solution)/shard_map/scatter | solution.py:53
  50.7 5.8 %all-to-all-start = ((s32[8,1,6]{2,1,0:T(1,128)}), s32[8,1,6]{2,1,0:T(1,128)S(1)}, u32[]{:S(2)}, u32[]{:S(2)}) async-start(s32[8,1,6]{2,1,0:T(1,128)} %bitcast.4), calls=%async_computation | async-start | bytes 8192 | tf_op jit(solution)/shard_map/all_to_all | solution.py:58
  56.6 35.0 %all-gather.2.cloned.1.call-done = bf16[8,768,512]{2,1,0:T(8,128)(2,1)} async-done(((bf16[8,768,128]{2,1,0:T(8,128)(2,1)}), bf16[8,768,512]{2,1,0:T(8,128)(2,1)}) %all-gather.2.cloned.1.call-update) | async-done | bytes 6291472 | tf_op jit(solution)/shard_map/all_gather | solution.py:35
  91.6 0.0 copy-done.2
  91.6 0.0 copy-done.3
  91.6 4.4 %fusion.5 = f32[8,128,512]{2,1,0:T(8,128)S(1)} fusion(bf16[8,768,512]{2,1,0:T(8,128)(2,1)} %all-gather.2.cloned.1.call-done, bf16[8,768,128]{2,1,0:T(8,128)(2,1)S(1)} %copy-done.2, f32[8,768]{1,0:T(8,128)S(1)} %copy-done.3), kind=kOutput, calls=%fused_computation.9 | convolution fusion | flops 807665664 | bytes 9986048 | tf_op jit(solution)/shard_map/snr,snc->src/dot_general | solution.py:32
  96.0 0.2 fusion.15
  96.2 1.5 pad_maximum_fusion
  97.7 2.0 %broadcast_in_dim.31 = f32[8,6,128,128]{3,2,1,0:T(8,128)} broadcast(f32[]{:T(128)} %constant.19.clone.1), dimensions={} | broadcast | bytes 3145732 | tf_op jit(solution)/shard_map/broadcast_in_dim | solution.py:50
  99.7 6.5 %scatter_fusion.1 = f32[8,6,128,128]{3,2,1,0:T(8,128)} fusion(f32[8,6,128,128]{3,2,1,0:T(8,128)} %broadcast_in_dim.31, s32[32]{0:T(128)S(1)} %reshape.125, f32[32,128,128]{2,1,0:T(8,128)} %bitcast.32), kind=kCustom, calls=%fused_computation.1 | custom fusion | bytes 6291712 | tf_op jit(solution)/shard_map/scatter | solution.py:51
  106.3 3.3 %convert_element_type.33 = bf16[8,6,128,128]{3,2,1,0:T(8,128)(2,1)} convert(f32[8,6,128,128]{3,2,1,0:T(8,128)} %scatter_fusion.1) | non-fusion elementwise | flops 786432 | bytes 4718592 | tf_op jit(solution)/shard_map/convert_element_type | solution.py:56
  109.6 0.0 all-to-all-done
  109.6 5.8 %all-to-all-start.1 = ((bf16[8,6,128,128]{3,2,1,0:T(8,128)(2,1)}), bf16[8,6,128,128]{3,2,1,0:T(8,128)(2,1)S(1)}, u32[]{:S(2)}, u32[]{:S(2)}) async-start(bf16[8,6,128,128]{3,2,1,0:T(8,128)(2,1)} %convert_element_type.33), calls=%async_computation.1 | async-start | bytes 3145728 | tf_op jit(solution)/shard_map/all_to_all | solution.py:55
  115.4 0.5 broadcast.141
  115.9 0.7 reduce.3
  116.5 0.1 reshape.117
  116.6 36.1 %all-to-all-done.1 = bf16[8,6,128,128]{3,2,1,0:T(8,128)(2,1)S(1)} async-done(((bf16[8,6,128,128]{3,2,1,0:T(8,128)(2,1)}), bf16[8,6,128,128]{3,2,1,0:T(8,128)(2,1)S(1)}, u32[]{:S(2)}, u32[]{:S(2)}) %all-to-all-start.1) | async-done | bytes 1572896 | tf_op jit(solution)/shard_map/all_to_all | solution.py:55
  152.8 2.1 %bitcast_convert_fusion = f32[48,128,128]{2,1,0:T(8,128)} fusion(bf16[8,6,128,128]{3,2,1,0:T(8,128)(2,1)S(1)} %all-to-all-done.1), kind=kLoop, calls=%fused_computation.10 | loop fusion | flops 786432 | bytes 4718592 | tf_op jit(solution)/shard_map/reshape | solution.py:62
  154.9 4.3 %broadcast_in_dim.28 = f32[129,128,128]{2,1,0:T(8,128)} broadcast(f32[]{:T(128)} %constant.19.clone.1), dimensions={} | broadcast | bytes 8454148 | tf_op jit(solution)/shard_map/broadcast_in_dim | solution.py:60
  159.2 10.2 %scatter_fusion.2 = f32[129,128,128]{2,1,0:T(8,128)} fusion(f32[129,128,128]{2,1,0:T(8,128)} %broadcast_in_dim.28, s32[48]{0:T(128)S(1)} %fusion.14, f32[48,128,128]{2,1,0:T(8,128)} %bitcast_convert_fusion), kind=kCustom, calls=%fused_computation.2 | custom fusion | flops 786432 | bytes 9437376 | tf_op jit(solution)/shard_map/scatter-add | solution.py:61
  169.5 4.0 %slice.16 = f32[128,128,128]{2,1,0:T(8,128)S(1)} slice(f32[129,128,128]{2,1,0:T(8,128)} %scatter_fusion.2), slice={[0:128], [0:128], [0:128]} | slice | bytes 16777216 | tf_op jit(solution)/shard_map/slice | solution.py:67
  173.4 0.0 dynamic-slice-start
  173.4 6.5 %copy.39 = f32[16,128,8,128]{3,2,1,0:T(8,128)S(1)} copy(f32[16,128,8,128]{3,1,2,0:T(8,128)S(1)} %bitcast.31) | data formatting | bytes 16777216 | tf_op jit(solution)/shard_map/transpose | solution.py:66
  180.0 0.0 dynamic-slice-done
  180.0 0.0 copy-start.1
  180.0 4.2 %bitcast_add_fusion = f32[2048,1024]{1,0:T(8,128)} fusion(f32[256,8,8,128]{3,2,1,0:T(8,128)S(1)} %bitcast.30, f32[2048]{0:T(1024)S(1)} %dynamic-slice-done, s32[1024]{0:T(1024)S(1)} %iota_add_fusion.1, s32[2048]{0:T(1024)S(1)} %iota_add_fusion), kind=kLoop, calls=%fused_computation.5 | loop fusion | flops 6291456 | bytes 16797696 | tf_op jit(solution)/shard_map/add | solution.py:76
  184.2 0.0 copy-done.1
  (9 shorter events, 0.1 us)
Async XLA Ops:
  6.5 27.5 %copy-start = (bf16[8,768,128]{2,1,0:T(8,128)(2,1)S(1)}, bf16[8,768,128]{2,1,0:T(8,128)(2,1)}, u32[]{:S(2)}) copy-start(bf16[8,768,128]{2,1,0:T(8,128)(2,1)} %param.8) | copy-start | bytes 4718596
  6.5 85.1 %all-gather.2.cloned.1.call-start = ((), (), s32[]{:S(2)}) async-start(), calls=%async_computation.2 | async-start | bytes 7864320 | tf_op jit(solution)/shard_map/all_gather | solution.py:35
  34.0 10.2 %copy-start.4 = (s32[8,4]{0,1:T(4,128)S(1)}, s32[8,4]{0,1:T(4,128)}, u32[]{:S(2)}) copy-start(s32[8,4]{0,1:T(4,128)} %param.10) | copy-start | bytes 388
  45.4 46.2 %copy-start.2 = (bf16[8,768,128]{2,1,0:T(8,128)(2,1)S(1)}, bf16[8,768,128]{2,1,0:T(8,128)(2,1)}, u32[]{:S(2)}) copy-start(bf16[8,768,128]{2,1,0:T(8,128)(2,1)} %fusion.2) | copy-start | bytes 4718596
  45.4 46.2 %copy-start.3 = (f32[8,768]{1,0:T(8,128)S(1)}, f32[8,768]{1,0:T(8,128)}, u32[]{:S(2)}) copy-start(f32[8,768]{1,0:T(8,128)} %param.9) | copy-start | bytes 73732
  50.7 58.8 %all-to-all-start = ((s32[8,1,6]{2,1,0:T(1,128)}), s32[8,1,6]{2,1,0:T(1,128)S(1)}, u32[]{:S(2)}, u32[]{:S(2)}) async-start(s32[8,1,6]{2,1,0:T(1,128)} %bitcast.4), calls=%async_computation | async-start | bytes 8192 | tf_op jit(solution)/shard_map/all_to_all | solution.py:58
  109.6 43.2 %all-to-all-start.1 = ((bf16[8,6,128,128]{3,2,1,0:T(8,128)(2,1)}), bf16[8,6,128,128]{3,2,1,0:T(8,128)(2,1)S(1)}, u32[]{:S(2)}, u32[]{:S(2)}) async-start(bf16[8,6,128,128]{3,2,1,0:T(8,128)(2,1)} %convert_element_type.33), calls=%async_computation.1 | async-start | bytes 3145728 | tf_op jit(solution)/shard_map/all_to_all | solution.py:55
  173.4 6.6 %dynamic-slice-start = ((f32[8192]{0:T(1024)}, s32[]{:T(128)}), f32[2048]{0:T(1024)S(1)}, s32[]{:S(2)}) async-start(f32[8192]{0:T(1024)} %param.11, s32[]{:T(128)} %select_n.58), calls=%async_computation.3 | async-start | bytes 16896 | tf_op jit(solution)/shard_map/dynamic_slice | solution.py:74
  180.0 4.2 %copy-start.1 = (bf16[8,768,128]{2,1,0:T(8,128)(2,1)S(1)}, bf16[8,768,128]{2,1,0:T(8,128)(2,1)}, u32[]{:S(2)}) copy-start(bf16[8,768,128]{2,1,0:T(8,128)(2,1)} %param.8) | copy-start | bytes 4718596
Sparse Core Ops, SparseCore 0:
  44.3 47.2 all-gather.1
where the time goes:
time: 194 us; the launch traced here: 191 us
  waiting for transfers between devices  71.2 us (37%)
  local copies, waits for them, and re-layouts  57.1 us (29%)
  other arithmetic  23.2 us (12%)
  matrix products  14.5 us (7%)
  between operations  13.5 us (7%)
  starting transfers between devices  11.6 us (6%)
    all_to_all x1, waiting for transfers between devices, on_device(): lax.all_to_all(send_blocks.astype(jnp.bfloat16), 'scen', split_axis=0, co...  36.1 us
    all_gather x1, waiting for transfers between devices, on_device(): lax.all_gather(solved_own, 'tile', axis=2, tiled=True)  35 us
    mul x2, local copies, waits for them, and re-layouts, on_device(): shaped * effective[:, :, None, :, None].astype(jnp.bfloat16)  26.6 us
    scatter-add x1, other arithmetic, on_device(): target_bins.at[received_targets.reshape(-1)]  10.2 us
    dot_general x1, matrix products, on_device(): jnp.einsum('snm,smc->snc', masked, border, preferred_element_type=jnp.flo...  10.1 us
    transpose x1, local copies, waits for them, and re-layouts, on_device(): jnp.transpose(target_bins[:bin_count].reshape(group_blocks, owner_blocks,...  6.54 us
    scatter x1, local copies, waits for them, and re-layouts, on_device(): send_blocks = send_blocks.at[destination, slot_rank].set(blocks_out)  6.51 us
    all_to_all x1, starting transfers between devices, on_device(): lax.all_to_all(send_targets, 'scen', split_axis=0, concat_axis=0, tiled=T...  5.84 us
  transfers between devices with their start and end apart: 3, of which 2 were waited for; matrix products, arithmetic and copies ran while one was open for 13% of the time, Pallas kernels for 0%

commit v1 on v0

--- a/solution.py
+++ b/solution.py
@@ -1,10 +1,14 @@
+import functools
+
 import jax
 import jax.numpy as jnp
 from jax import lax
+from jax.experimental import pallas as pl
+from jax.experimental.pallas import tpu as pltpu
 from jax.sharding import PartitionSpec as P
 
 
-def on_device(factor_inv, pattern, border, row_scale, link_ids, first_diag):
+def general_form(factor_inv, pattern, border, row_scale, link_ids, first_diag):
     local_scen, scen_rows, _ = factor_inv.shape
     block_count = pattern.shape[1]
     block_size = border.shape[2]
@@ -76,6 +80,352 @@
     return tile_out + jnp.where(on_diagonal, diag_values[:, None], 0.0)
 
 
+MESH = pl.DeviceIdType.MESH
+BF16 = jnp.bfloat16
+F32 = jnp.float32
+
+
+def wait_bytes(ref, sem):
+    pltpu.make_async_copy(ref, ref, sem).wait()
+
+
+def loop(count, body):
+    def step(i, carry):
+        body(i)
+        return carry
+
+    lax.fori_loop(0, count, step, 0)
+
+
+def exchange_kernel(
+    nblk, bs, pat_ref, scale_ref, link_ref, factor_ref, border_ref,
+    recv_ref, links_ref,
+    fbuf, bbuf, own, sib, far, near_out, cross_out,
+    f_sem, b_sem, sib_send, sib_recv, far_send, far_recv,
+    near_send, cross_send, rcv, fw_send, fw_recv, lk_send, lk_recv,
+):
+    scen = lax.axis_index("scen")
+    tile = lax.axis_index("tile")
+    zz, yy = scen // 2, scen % 2
+    xx, cc = tile // 2, tile % 2
+    xo = 1 - xx
+    mate = 2 * xx + 1 - cc
+
+    def ordered(m):
+        half, rest = m // 4, m % 4
+        chip = lax.rem(xo + half, 2)
+        return 2 * chip + rest % 2 + 4 * (rest // 2)
+
+    def load(m):
+        s = ordered(m)
+        pltpu.make_async_copy(factor_ref.at[s], fbuf.at[s], f_sem.at[s]).start()
+        pltpu.make_async_copy(border_ref.at[s], bbuf.at[s], b_sem.at[s]).start()
+
+    loop(8, load)
+
+    barrier = pltpu.get_barrier_semaphore()
+
+    def greet(k):
+        place = lax.rem(zz * 4 + tile + k + 1, 16)
+        pl.semaphore_signal(
+            barrier, inc=1, device_id=(2 * (place // 4) + yy, place % 4), device_id_type=MESH
+        )
+
+    def greet_other(k):
+        pl.semaphore_signal(
+            barrier, inc=1, device_id=(2 * k + 1 - yy, tile), device_id_type=MESH
+        )
+
+    loop(15, greet)
+    loop(4, greet_other)
+    pl.semaphore_wait(barrier, 19)
+
+    def solve(s):
+        wait_bytes(fbuf.at[s], f_sem.at[s])
+        wait_bytes(bbuf.at[s], b_sem.at[s])
+        for a in range(nblk):
+            parts = []
+            for b in range(a):
+                keep = pat_ref[s, a, b].astype(F32)
+                block = fbuf[s, a * bs:(a + 1) * bs, b * bs:(b + 1) * bs]
+                parts.append((block.astype(F32) * keep).astype(BF16))
+            parts.append(fbuf[s, a * bs:(a + 1) * bs, a * bs:(a + 1) * bs])
+            left = parts[0] if a == 0 else jnp.concatenate(parts, axis=1)
+            out = jnp.dot(left, bbuf[s, :(a + 1) * bs, :], preferred_element_type=F32)
+            own[s, a * bs:(a + 1) * bs, :] = out.astype(BF16)
+
+    def to_mate(s):
+        return pltpu.make_async_remote_copy(
+            own.at[s], sib.at[s], sib_send.at[s], sib_recv.at[s],
+            device_id=(scen, mate), device_id_type=MESH,
+        )
+
+    def to_far(m):
+        s = ordered(m)
+        return pltpu.make_async_remote_copy(
+            own.at[s], far.at[m // 2, cc], far_send.at[m], far_recv.at[m // 2, cc],
+            device_id=(scen, 2 * xo + m % 2), device_id_type=MESH,
+        )
+
+    def first(m):
+        s = ordered(m)
+        solve(s)
+        to_far(m).start()
+        to_mate(s).start()
+
+    def second(m):
+        s = ordered(m + 4)
+        solve(s)
+        to_mate(s).start()
+
+    def turned(block, s):
+        return (block.astype(F32).T * scale_ref[pl.ds(s, 1), :]).astype(BF16)
+
+    def near_copy(half, s):
+        column = tile if half == 0 else mate
+        return column, pltpu.make_async_remote_copy(
+            near_out.at[half, s], recv_ref.at[scen, s], near_send.at[half, s], rcv.at[zz, s],
+            device_id=(2 * column + yy, tile), device_id_type=MESH,
+        )
+
+    def send_near(half, s):
+        column, copy = near_copy(half, s)
+
+        @pl.when(column != zz)
+        def _():
+            copy.start()
+
+        @pl.when(column == zz)
+        def _():
+            pltpu.make_async_copy(
+                near_out.at[half, s], recv_ref.at[scen, s], rcv.at[zz, s]
+            ).start()
+
+    def near(m):
+        s = ordered(m)
+        wait_bytes(sib.at[s], sib_recv.at[s])
+        right = jnp.concatenate([own[s], sib[s]], axis=1)
+        out = jnp.dot(turned(own[s], s), right, preferred_element_type=F32).astype(BF16)
+        near_out[0, s] = out[:, :bs]
+        near_out[1, s] = out[:, bs:]
+        send_near(0, s)
+        send_near(1, s)
+
+    def cross_copy(k, e):
+        s = tile + 4 * k
+        if e < 4:
+            row = tile if e // 2 == 0 else mate
+            column = 2 * xo + e % 2
+        else:
+            row = 2 * xo + (e - 4) // 2
+            column = tile if e % 2 == 0 else mate
+        return column, pltpu.make_async_remote_copy(
+            cross_out.at[k, e], recv_ref.at[scen, s], cross_send.at[k, e], rcv.at[zz, s],
+            device_id=(2 * column + yy, row), device_id_type=MESH,
+        )
+
+    def cross(k):
+        s = tile + 4 * k
+        wait_bytes(far.at[k, 0], far_recv.at[k, 0])
+        wait_bytes(far.at[k, 1], far_recv.at[k, 1])
+        here = jnp.concatenate([own[s], sib[s]], axis=1)
+        there = jnp.concatenate([far[k, 0], far[k, 1]], axis=1)
+        for way, (a, b) in enumerate(((here, there), (there, here))):
+            out = jnp.dot(turned(a, s), b, preferred_element_type=F32).astype(BF16)
+            for e in range(4):
+                i, j = e // 2, e % 2
+                cross_out[k, 4 * way + e] = out[i * bs:(i + 1) * bs, j * bs:(j + 1) * bs]
+        for e in range(7, -1, -1):
+            column, copy = cross_copy(k, e)
+            if e >= 2:
+                copy.start()
+            else:
+
+                @pl.when(column != zz)
+                def _():
+                    copy.start()
+
+                @pl.when(column == zz)
+                def _():
+                    pltpu.make_async_copy(
+                        cross_out.at[k, e], recv_ref.at[scen, s], rcv.at[zz, s]
+                    ).start()
+
+    def forward_copy(src, s):
+        slot = recv_ref.at[2 * src + yy, s]
+        return pltpu.make_async_remote_copy(
+            slot, slot, fw_send.at[src, s], fw_recv.at[src, s],
+            device_id=(2 * zz + 1 - yy, tile), device_id_type=MESH,
+        )
+
+    def forward(base, q):
+        s = base + q // 4
+        src = lax.rem(zz + q, 4)
+        wait_bytes(recv_ref.at[2 * src + yy, s], rcv.at[src, s])
+        forward_copy(src, s).start()
+
+    def link_copy(k):
+        other = lax.rem(scen + k + 1, 8)
+        return other, pltpu.make_async_remote_copy(
+            link_ref, links_ref.at[scen], lk_send.at[k], lk_recv.at[scen],
+            device_id=(other, tile), device_id_type=MESH,
+        )
+
+    loop(4, first)
+    loop(4, second)
+    loop(8, near)
+    pltpu.make_async_copy(link_ref, links_ref.at[scen], lk_recv.at[scen]).start()
+    loop(7, lambda k: link_copy(k)[1].start())
+    cross(0)
+    loop(16, functools.partial(forward, 0))
+    cross(1)
+    loop(16, functools.partial(forward, 4))
+
+    loop(8, lambda s: wait_bytes(own.at[s], sib_send.at[s]))
+    loop(4, lambda m: wait_bytes(own.at[m], far_send.at[m]))
+
+    def sent_near(s):
+        for half in range(2):
+            column, copy = near_copy(half, s)
+
+            @pl.when(column != zz)
+            def _():
+                copy.wait_send()
+
+    loop(8, sent_near)
+    for k in range(2):
+        for e in range(8):
+            column, copy = cross_copy(k, e)
+            if e >= 2:
+                copy.wait_send()
+            else:
+
+                @pl.when(column != zz)
+                def _():
+                    copy.wait_send()
+
+    loop(7, lambda k: link_copy(k)[1].wait_send())
+    loop(8, lambda p: wait_bytes(links_ref.at[p], lk_recv.at[p]))
+
+    def finish(q):
+        src, s = q % 4, q // 4
+        forward_copy(src, s).wait_send()
+        wait_bytes(recv_ref.at[2 * src + 1 - yy, s], fw_recv.at[src, s])
+
+    loop(32, finish)
+
+
+def assemble_kernel(
+    group_blocks, owner_blocks, bs, links_ref, recv_ref, diag_ref, out_ref, head, follow, place
+):
+    scen = lax.axis_index("scen")
+    tile = lax.axis_index("tile")
+    group = scen * owner_blocks // group_blocks
+    r = pl.program_id(0)
+    parts, each = recv_ref.shape[0], recv_ref.shape[1]
+
+    @pl.when(r == 0)
+    def _():
+        def clear(i, carry):
+            head[i] = -1
+            return carry
+
+        lax.fori_loop(0, group_blocks, clear, 0)
+
+        def enter(n, carry):
+            column = links_ref[n // each, n % each, group] - scen * owner_blocks
+
+            @pl.when(jnp.logical_and(column >= 0, column < owner_blocks))
+            def _():
+                row = links_ref[n // each, n % each, tile] - tile * group_blocks
+                follow[n] = head[row]
+                place[n] = column
+                head[row] = n
+
+            return carry
+
+        lax.fori_loop(0, parts * each, enter, 0)
+
+    out_ref[...] = jnp.zeros_like(out_ref)
+
+    def add(n):
+        at = pl.ds(pl.multiple_of(place[n] * bs, bs), bs)
+        out_ref[:, at] += recv_ref[n // each, n % each].astype(F32)
+        return follow[n]
+
+    lax.while_loop(lambda n: n >= 0, add, head[r])
+    block = tile * group_blocks + r
+    column = block - scen * owner_blocks
+
+    @pl.when(jnp.logical_and(column >= 0, column < owner_blocks))
+    def _():
+        at = pl.ds(pl.multiple_of(column * bs, bs), bs)
+        values = jnp.broadcast_to(diag_ref[pl.ds(block, 1), :], (bs, bs))
+        same = lax.broadcasted_iota(jnp.int32, (bs, bs), 0) == lax.broadcasted_iota(
+            jnp.int32, (bs, bs), 1
+        )
+        out_ref[:, at] += jnp.where(same, values, 0.0)
+
+
+def two_owner_form(factor_inv, pattern, border, row_scale, link_ids, first_diag):
+    local_scen, rows, _ = factor_inv.shape
+    nblk = pattern.shape[1]
+    bs = border.shape[2]
+    order = first_diag.shape[0]
+    tiles = lax.axis_size("tile")
+    owners = lax.axis_size("scen")
+    group_blocks = order // (tiles * bs)
+    owner_blocks = order // (owners * bs)
+    links = jnp.pad(link_ids, ((0, 0), (0, 128 - link_ids.shape[1])))
+    dma = pltpu.SemaphoreType.DMA
+    vmem = pl.BlockSpec(memory_space=pltpu.VMEM)
+    smem = pl.BlockSpec(memory_space=pltpu.SMEM)
+    hbm = pl.BlockSpec(memory_space=pl.ANY)
+    received, all_links = pl.pallas_call(
+        functools.partial(exchange_kernel, nblk, bs),
+        out_shape=(
+            jax.ShapeDtypeStruct((owners, local_scen, bs, bs), BF16),
+            jax.ShapeDtypeStruct((owners, local_scen, 128), jnp.int32),
+        ),
+        in_specs=[smem, vmem, vmem, hbm, hbm],
+        out_specs=(hbm, hbm),
+        scratch_shapes=[
+            pltpu.VMEM(factor_inv.shape, BF16),
+            pltpu.VMEM(border.shape, BF16),
+            pltpu.VMEM((8, rows, bs), BF16),
+            pltpu.VMEM((8, rows, bs), BF16),
+            pltpu.VMEM((2, 2, rows, bs), BF16),
+            pltpu.VMEM((2, 8, bs, bs), BF16),
+            pltpu.VMEM((2, 8, bs, bs), BF16),
+            dma((8,)), dma((8,)), dma((8,)), dma((8,)), dma((4,)), dma((2, 2)),
+            dma((2, 8)), dma((2, 8)), dma((4, 8)), dma((4, 8)), dma((4, 8)),
+            dma((7,)), dma((8,)),
+        ],
+        compiler_params=pltpu.CompilerParams(
+            collective_id=0, has_side_effects=True, vmem_limit_bytes=40 * 1024 * 1024
+        ),
+    )(pattern, row_scale, links, factor_inv, border)
+    return pl.pallas_call(
+        functools.partial(assemble_kernel, group_blocks, owner_blocks, bs),
+        out_shape=jax.ShapeDtypeStruct((group_blocks * bs, owner_blocks * bs), F32),
+        grid=(group_blocks,),
+        in_specs=[smem, vmem, vmem],
+        out_specs=pl.BlockSpec((bs, owner_blocks * bs), lambda r: (r, 0)),
+        scratch_shapes=[
+            pltpu.SMEM((group_blocks,), jnp.int32),
+            pltpu.SMEM((owners * local_scen,), jnp.int32),
+            pltpu.SMEM((owners * local_scen,), jnp.int32),
+        ],
+        compiler_params=pltpu.CompilerParams(vmem_limit_bytes=24 * 1024 * 1024),
+    )(all_links, received, first_diag.reshape(order // bs, bs))
+
+
+def on_device(factor_inv, *rest):
+    sizes = (lax.axis_size("tile"), lax.axis_size("scen"), factor_inv.shape[0])
+    form = two_owner_form if sizes == (4, 8, 8) else general_form
+    return form(factor_inv, *rest)
+
+
 def solution(mesh):
     in_specs = (
         P("scen", None, None),

time: 194 us -> 85.3 us (0.44); the launches traced: 191 us -> 84.9 us
  Pallas kernels: 0 us -> 77.5 us
  waiting for transfers between devices: 71.2 us -> 0 us
  local copies, waits for them, and re-layouts: 57.1 us -> 7.34 us
  other arithmetic: 23.2 us -> 0 us
  matrix products: 14.5 us -> 0 us
  between operations: 13.5 us -> 0.02 us
  starting transfers between devices: 11.6 us -> 0 us
    pallas_call x0 -> x2, Pallas kernels: none -> 77.5 us  [the longest x1 67.4 us: two_owner_form(): pl.pallas_call(functools.partial(exchange_kernel, nblk, bs), out_shape=(j...]
    all_to_all x2 -> x0, waiting for transfers between devices: 36.1 us -> none  [the longest x1 36.1 us: on_device(): lax.all_to_all(send_blocks.astype(jnp.bfloat16), 'scen', split_axis=0, co...]
    all_gather x1 -> x0, waiting for transfers between devices: 35 us -> none  [on_device(): lax.all_gather(solved_own, 'tile', axis=2, tiled=True)]
    mul x2 -> x0, local copies, waits for them, and re-layouts: 26.6 us -> none  [on_device(): shaped * effective[:, :, None, :, None].astype(jnp.bfloat16)]
    dot_general x2 -> x0, matrix products: 14.5 us -> none  [the longest x1 10.1 us: on_device(): jnp.einsum('snm,smc->snc', masked, border, preferred_element_type=jnp.flo...]
    scatter x2 -> x0, local copies, waits for them, and re-layouts: 11.9 us -> none  [the longest x1 6.51 us: on_device(): send_blocks = send_blocks.at[destination, slot_rank].set(blocks_out)]
    all_to_all x2 -> x0, starting transfers between devices: 11.6 us -> none  [the longest x1 5.84 us: on_device(): lax.all_to_all(send_targets, 'scen', split_axis=0, concat_axis=0, tiled=T...]
    scatter-add x1 -> x0, other arithmetic: 10.2 us -> none  [on_device(): target_bins.at[received_targets.reshape(-1)]]
  transfers between devices with their start and end apart: 3 -> 0, of which waited for: 2 -> 0; matrix products, arithmetic and copies ran while one was open for 13% -> 0% of each run, Pallas kernels for 0% -> 0%
where the time goes in v1:
time: 85.3 us; the launch traced here: 84.9 us
  Pallas kernels  77.5 us (91%)
  local copies, waits for them, and re-layouts  7.34 us (9%)
    pallas_call x1, Pallas kernels, two_owner_form(): pl.pallas_call(functools.partial(exchange_kernel, nblk, bs), out_shape=(j...  67.4 us
    pallas_call x1, Pallas kernels, two_owner_form(): pl.pallas_call(functools.partial(assemble_kernel, group_blocks, owner_blo...  10.2 us
    unnamed x10, local copies, waits for them, and re-layouts  7.33 us

profile of v1, /device:TPU:2, one launch (start us, length us, event | category | flops | bytes accessed | tf_op | source)
XLA Modules:
  0.0 84.9 jit_solution(2959879130419695249)
XLA Ops:
  0.0 0.0 copy-start.2
  0.0 0.8 copy.7
  0.8 0.7 copy.8.pat_ref
  1.5 0.0 copy-start
  1.5 3.7 %copy-done = bf16[8,768,768]{2,1,0:T(8,128)(2,1)S(1)} copy-done((bf16[8,768,768]{2,1,0:T(8,128)(2,1)S(1)}, bf16[8,768,768]{2,1,0:T(8,128)(2,1)}, u32[]{:S(2)}) %copy-start) | copy-done | bytes 9437208
  5.2 0.0 copy-start.1
  5.2 1.4 %copy-done.1 = bf16[8,768,128]{2,1,0:T(8,128)(2,1)S(1)} copy-done((bf16[8,768,128]{2,1,0:T(8,128)(2,1)S(1)}, bf16[8,768,128]{2,1,0:T(8,128)(2,1)}, u32[]{:S(2)}) %copy-start.1) | copy-done | bytes 1572888
  6.6 0.0 copy-start.3
  6.6 0.7 copy-done.3
  7.3 67.4 %shard_map.64 = (bf16[8,8,128,128]{3,2,1,0:T(8,128)(2,1)S(1)}, s32[8,8,128]{2,1,0:T(8,128)S(1)}) custom-call(s32[8,6,6]{2,1,0:T(8,128)S(1)} %copy.8.pat_ref, f32[8,768]{1,0:T(8,128)S(1)} %copy-done.3, s32[8,128]{1,0:T(8,128)S(1)} %pad.4.link_ref, bf16[8,768,768]{2,1,0:T(8,128)(2,1)S(1)} %copy-done, bf16[8,768,128]{2,1,0:T(8,128)(2,1)S(1)} %copy-done.1), custom_call_target="tpu_custom_call" | custom-call | tf_op jit(solution)/shard_map/pallas_call | solution.py:384
  74.7 0.0 copy-done.2
  74.7 10.2 %shard_map.65 = f32[2048,1024]{1,0:T(8,128)} custom-call(s32[8,8,128]{2,1,0:T(8,128)S(1)} %get-tuple-element.7.links_ref, bf16[8,8,128,128]{3,2,1,0:T(8,128)(2,1)S(1)} %get-tuple-element.8.recv_ref, f32[64,128]{1,0:T(8,128)S(1)} %bitcast.1), custom_call_target="tpu_custom_call" | custom-call | tf_op jit(solution)/shard_map/pallas_call | solution.py:408
  (1 shorter events, 0.0 us)
Async XLA Ops:
  0.0 74.7 %copy-start.2 = (f32[8192]{0:T(1024)S(1)}, f32[8192]{0:T(1024)}, u32[]{:S(2)}) copy-start(f32[8192]{0:T(1024)} %param.11) | copy-start | bytes 98308
  1.5 3.7 %copy-start = (bf16[8,768,768]{2,1,0:T(8,128)(2,1)S(1)}, bf16[8,768,768]{2,1,0:T(8,128)(2,1)}, u32[]{:S(2)}) copy-start(bf16[8,768,768]{2,1,0:T(8,128)(2,1)} %factor_ref.1) | copy-start | bytes 28311556
  5.2 1.4 %copy-start.1 = (bf16[8,768,128]{2,1,0:T(8,128)(2,1)S(1)}, bf16[8,768,128]{2,1,0:T(8,128)(2,1)}, u32[]{:S(2)}) copy-start(bf16[8,768,128]{2,1,0:T(8,128)(2,1)} %border_ref.1) | copy-start | bytes 4718596
  6.6 0.7 copy-start.3

commit v2 on v1

--- a/solution.py
+++ b/solution.py
@@ -143,16 +143,26 @@
     def solve(s):
         wait_bytes(fbuf.at[s], f_sem.at[s])
         wait_bytes(bbuf.at[s], b_sem.at[s])
-        for a in range(nblk):
-            parts = []
-            for b in range(a):
-                keep = pat_ref[s, a, b].astype(F32)
-                block = fbuf[s, a * bs:(a + 1) * bs, b * bs:(b + 1) * bs]
-                parts.append((block.astype(F32) * keep).astype(BF16))
-            parts.append(fbuf[s, a * bs:(a + 1) * bs, a * bs:(a + 1) * bs])
-            left = parts[0] if a == 0 else jnp.concatenate(parts, axis=1)
-            out = jnp.dot(left, bbuf[s, :(a + 1) * bs, :], preferred_element_type=F32)
-            own[s, a * bs:(a + 1) * bs, :] = out.astype(BF16)
+        total = None
+        for first_col in range(0, nblk, 2):
+            lines = []
+            for a in range(first_col, nblk):
+                parts = []
+                for b in range(first_col, first_col + 2):
+                    block = fbuf[s, a * bs:(a + 1) * bs, b * bs:(b + 1) * bs]
+                    if b < a:
+                        keep = pat_ref[a, s, b].astype(F32)
+                        block = (block.astype(F32) * keep).astype(BF16)
+                    elif b > a:
+                        block = jnp.zeros((bs, bs), BF16)
+                    parts.append(block)
+                lines.append(jnp.concatenate(parts, axis=1))
+            right = bbuf[s, first_col * bs:(first_col + 2) * bs, :]
+            out = jnp.dot(jnp.concatenate(lines, axis=0), right, preferred_element_type=F32)
+            if total is not None:
+                out = out + total[2 * bs:]
+            own[s, first_col * bs:(first_col + 2) * bs, :] = out[:2 * bs].astype(BF16)
+            total = out
 
     def to_mate(s):
         return pltpu.make_async_remote_copy(
@@ -167,49 +177,49 @@
             device_id=(scen, 2 * xo + m % 2), device_id_type=MESH,
         )
 
-    def first(m):
-        s = ordered(m)
-        solve(s)
-        to_far(m).start()
-        to_mate(s).start()
-
-    def second(m):
-        s = ordered(m + 4)
-        solve(s)
-        to_mate(s).start()
+    def first(k):
+        for m in (2 * k, 2 * k + 1):
+            solve(ordered(m))
+            to_far(m).start()
+            to_mate(ordered(m)).start()
+
+    def second(k):
+        for m in (2 * k + 4, 2 * k + 5):
+            solve(ordered(m))
+            to_mate(ordered(m)).start()
 
     def turned(block, s):
-        return (block.astype(F32).T * scale_ref[pl.ds(s, 1), :]).astype(BF16)
-
-    def near_copy(half, s):
+        return (block.T.astype(F32) * scale_ref[pl.ds(s, 1), :]).astype(BF16)
+
+    def near_copy(half, p):
         column = tile if half == 0 else mate
+        two = pl.ds(2 * p, 2)
         return column, pltpu.make_async_remote_copy(
-            near_out.at[half, s], recv_ref.at[scen, s], near_send.at[half, s], rcv.at[zz, s],
+            near_out.at[half, two], recv_ref.at[scen, two], near_send.at[half, p], rcv.at[zz, p],
             device_id=(2 * column + yy, tile), device_id_type=MESH,
         )
 
-    def send_near(half, s):
-        column, copy = near_copy(half, s)
-
-        @pl.when(column != zz)
-        def _():
-            copy.start()
-
-        @pl.when(column == zz)
-        def _():
-            pltpu.make_async_copy(
-                near_out.at[half, s], recv_ref.at[scen, s], rcv.at[zz, s]
-            ).start()
-
-    def near(m):
-        s = ordered(m)
-        wait_bytes(sib.at[s], sib_recv.at[s])
-        right = jnp.concatenate([own[s], sib[s]], axis=1)
-        out = jnp.dot(turned(own[s], s), right, preferred_element_type=F32).astype(BF16)
-        near_out[0, s] = out[:, :bs]
-        near_out[1, s] = out[:, bs:]
-        send_near(0, s)
-        send_near(1, s)
+    def near(h):
+        p = lax.rem(xo + h // 2, 2) + 2 * (h % 2)
+        for s in (2 * p, 2 * p + 1):
+            wait_bytes(sib.at[s], sib_recv.at[s])
+            right = jnp.concatenate([own[s], sib[s]], axis=1)
+            out = jnp.dot(turned(own[s], s), right, preferred_element_type=F32).astype(BF16)
+            near_out[0, s] = out[:, :bs]
+            near_out[1, s] = out[:, bs:]
+        for half in range(2):
+            column, copy = near_copy(half, p)
+
+            @pl.when(column != zz)
+            def _():
+                copy.start()
+
+            @pl.when(column == zz)
+            def _():
+                two = pl.ds(2 * p, 2)
+                pltpu.make_async_copy(
+                    near_out.at[half, two], recv_ref.at[scen, two], rcv.at[zz, p]
+                ).start()
 
     def cross_copy(k, e):
         s = tile + 4 * k
@@ -220,7 +230,7 @@
             row = 2 * xo + (e - 4) // 2
             column = tile if e % 2 == 0 else mate
         return column, pltpu.make_async_remote_copy(
-            cross_out.at[k, e], recv_ref.at[scen, s], cross_send.at[k, e], rcv.at[zz, s],
+            cross_out.at[k, e], recv_ref.at[scen, s], cross_send.at[k, e], rcv.at[zz, 2 * k + tile // 2],
             device_id=(2 * column + yy, row), device_id_type=MESH,
         )
 
@@ -248,21 +258,24 @@
                 @pl.when(column == zz)
                 def _():
                     pltpu.make_async_copy(
-                        cross_out.at[k, e], recv_ref.at[scen, s], rcv.at[zz, s]
+                        cross_out.at[k, e], recv_ref.at[scen, s], rcv.at[zz, 2 * k + tile // 2]
                     ).start()
 
-    def forward_copy(src, s):
-        slot = recv_ref.at[2 * src + yy, s]
+    def forward_copy(src, p):
+        slot = recv_ref.at[2 * src + yy, pl.ds(2 * p, 2)]
         return pltpu.make_async_remote_copy(
-            slot, slot, fw_send.at[src, s], fw_recv.at[src, s],
+            slot, slot, fw_send.at[src, p], fw_recv.at[src, p],
             device_id=(2 * zz + 1 - yy, tile), device_id_type=MESH,
         )
 
-    def forward(base, q):
-        s = base + q // 4
+    def forward(near_type, part, q):
+        if near_type:
+            p = lax.rem(xo + part, 2) + 2 * (q // 4)
+        else:
+            p = 2 * part + q // 4
         src = lax.rem(zz + q, 4)
-        wait_bytes(recv_ref.at[2 * src + yy, s], rcv.at[src, s])
-        forward_copy(src, s).start()
+        wait_bytes(recv_ref.at[2 * src + yy, pl.ds(2 * p, 2)], rcv.at[src, p])
+        forward_copy(src, p).start()
 
     def link_copy(k):
         other = lax.rem(scen + k + 1, 8)
@@ -271,28 +284,45 @@
             device_id=(other, tile), device_id_type=MESH,
         )
 
-    loop(4, first)
-    loop(4, second)
-    loop(8, near)
+    loop(2, first)
+    loop(2, near)
+    loop(2, second)
+    loop(2, lambda h: near(h + 2))
+
+    @pl.when(zz // 2 == xx)
+    def _():
+        loop(8, functools.partial(forward, True, 0))
+
+    cross(0)
+
+    @pl.when(zz // 2 == xx)
+    def _():
+        loop(8, functools.partial(forward, True, 1))
+
+    @pl.when(zz // 2 != xx)
+    def _():
+        loop(8, functools.partial(forward, False, 0))
+
+    cross(1)
     pltpu.make_async_copy(link_ref, links_ref.at[scen], lk_recv.at[scen]).start()
     loop(7, lambda k: link_copy(k)[1].start())
-    cross(0)
-    loop(16, functools.partial(forward, 0))
-    cross(1)
-    loop(16, functools.partial(forward, 4))
+
+    @pl.when(zz // 2 != xx)
+    def _():
+        loop(8, functools.partial(forward, False, 1))
 
     loop(8, lambda s: wait_bytes(own.at[s], sib_send.at[s]))
     loop(4, lambda m: wait_bytes(own.at[m], far_send.at[m]))
 
-    def sent_near(s):
+    def sent_near(p):
         for half in range(2):
-            column, copy = near_copy(half, s)
+            column, copy = near_copy(half, p)
 
             @pl.when(column != zz)
             def _():
                 copy.wait_send()
 
-    loop(8, sent_near)
+    loop(4, sent_near)
     for k in range(2):
         for e in range(8):
             column, copy = cross_copy(k, e)
@@ -308,11 +338,11 @@
     loop(8, lambda p: wait_bytes(links_ref.at[p], lk_recv.at[p]))
 
     def finish(q):
-        src, s = q % 4, q // 4
-        forward_copy(src, s).wait_send()
-        wait_bytes(recv_ref.at[2 * src + 1 - yy, s], fw_recv.at[src, s])
-
-    loop(32, finish)
+        src, p = q % 4, q // 4
+        forward_copy(src, p).wait_send()
+        wait_bytes(recv_ref.at[2 * src + 1 - yy, pl.ds(2 * p, 2)], fw_recv.at[src, p])
+
+    loop(16, finish)
 
 
 def assemble_kernel(
@@ -321,50 +351,51 @@
     scen = lax.axis_index("scen")
     tile = lax.axis_index("tile")
     group = scen * owner_blocks // group_blocks
-    r = pl.program_id(0)
+    first = pl.program_id(0) * (out_ref.shape[0] // bs)
     parts, each = recv_ref.shape[0], recv_ref.shape[1]
 
-    @pl.when(r == 0)
+    @pl.when(first == 0)
     def _():
-        def clear(i, carry):
+        for i in range(group_blocks):
             head[i] = -1
+
+        def enter(p, carry):
+            for s in range(each):
+                column = links_ref[p, group, s] - scen * owner_blocks
+                n = p * each + s
+
+                @pl.when(jnp.logical_and(column >= 0, column < owner_blocks))
+                def _():
+                    row = links_ref[p, tile, s] - tile * group_blocks
+                    follow[n] = head[row]
+                    place[n] = column
+                    head[row] = n
+
             return carry
 
-        lax.fori_loop(0, group_blocks, clear, 0)
-
-        def enter(n, carry):
-            column = links_ref[n // each, n % each, group] - scen * owner_blocks
-
-            @pl.when(jnp.logical_and(column >= 0, column < owner_blocks))
-            def _():
-                row = links_ref[n // each, n % each, tile] - tile * group_blocks
-                follow[n] = head[row]
-                place[n] = column
-                head[row] = n
-
-            return carry
-
-        lax.fori_loop(0, parts * each, enter, 0)
+        lax.fori_loop(0, parts, enter, 0)
 
     out_ref[...] = jnp.zeros_like(out_ref)
-
-    def add(n):
-        at = pl.ds(pl.multiple_of(place[n] * bs, bs), bs)
-        out_ref[:, at] += recv_ref[n // each, n % each].astype(F32)
-        return follow[n]
-
-    lax.while_loop(lambda n: n >= 0, add, head[r])
-    block = tile * group_blocks + r
-    column = block - scen * owner_blocks
-
-    @pl.when(jnp.logical_and(column >= 0, column < owner_blocks))
-    def _():
-        at = pl.ds(pl.multiple_of(column * bs, bs), bs)
-        values = jnp.broadcast_to(diag_ref[pl.ds(block, 1), :], (bs, bs))
-        same = lax.broadcasted_iota(jnp.int32, (bs, bs), 0) == lax.broadcasted_iota(
-            jnp.int32, (bs, bs), 1
-        )
-        out_ref[:, at] += jnp.where(same, values, 0.0)
+    same = lax.broadcasted_iota(jnp.int32, (bs, bs), 0) == lax.broadcasted_iota(
+        jnp.int32, (bs, bs), 1
+    )
+    for i in range(out_ref.shape[0] // bs):
+        rows = slice(i * bs, (i + 1) * bs)
+
+        def add(n):
+            at = pl.ds(pl.multiple_of(place[n] * bs, bs), bs)
+            out_ref[rows, at] += recv_ref[n // each, n % each].astype(F32)
+            return follow[n]
+
+        lax.while_loop(lambda n: n >= 0, add, head[first + i])
+        block = tile * group_blocks + first + i
+        column = block - scen * owner_blocks
+
+        @pl.when(jnp.logical_and(column >= 0, column < owner_blocks))
+        def _():
+            at = pl.ds(pl.multiple_of(column * bs, bs), bs)
+            values = jnp.broadcast_to(diag_ref[pl.ds(block, 1), :], (bs, bs))
+            out_ref[rows, at] += jnp.where(same, values, 0.0)
 
 
 def two_owner_form(factor_inv, pattern, border, row_scale, link_ids, first_diag):
@@ -376,7 +407,7 @@
     owners = lax.axis_size("scen")
     group_blocks = order // (tiles * bs)
     owner_blocks = order // (owners * bs)
-    links = jnp.pad(link_ids, ((0, 0), (0, 128 - link_ids.shape[1])))
+    links = jnp.pad(link_ids.T, ((0, 8 - link_ids.shape[1]), (0, 128 - local_scen)))
     dma = pltpu.SemaphoreType.DMA
     vmem = pl.BlockSpec(memory_space=pltpu.VMEM)
     smem = pl.BlockSpec(memory_space=pltpu.SMEM)
@@ -385,7 +416,7 @@
         functools.partial(exchange_kernel, nblk, bs),
         out_shape=(
             jax.ShapeDtypeStruct((owners, local_scen, bs, bs), BF16),
-            jax.ShapeDtypeStruct((owners, local_scen, 128), jnp.int32),
+            jax.ShapeDtypeStruct((owners, 8, 128), jnp.int32),
         ),
         in_specs=[smem, vmem, vmem, hbm, hbm],
         out_specs=(hbm, hbm),
@@ -398,19 +429,19 @@
             pltpu.VMEM((2, 8, bs, bs), BF16),
             pltpu.VMEM((2, 8, bs, bs), BF16),
             dma((8,)), dma((8,)), dma((8,)), dma((8,)), dma((4,)), dma((2, 2)),
-            dma((2, 8)), dma((2, 8)), dma((4, 8)), dma((4, 8)), dma((4, 8)),
+            dma((2, 4)), dma((2, 8)), dma((4, 4)), dma((4, 4)), dma((4, 4)),
             dma((7,)), dma((8,)),
         ],
         compiler_params=pltpu.CompilerParams(
-            collective_id=0, has_side_effects=True, vmem_limit_bytes=40 * 1024 * 1024
+            collective_id=0, has_side_effects=True, vmem_limit_bytes=62 * 1024 * 1024
         ),
-    )(pattern, row_scale, links, factor_inv, border)
+    )(jnp.transpose(pattern, (1, 0, 2)), row_scale, links, factor_inv, border)
     return pl.pallas_call(
         functools.partial(assemble_kernel, group_blocks, owner_blocks, bs),
         out_shape=jax.ShapeDtypeStruct((group_blocks * bs, owner_blocks * bs), F32),
-        grid=(group_blocks,),
+        grid=(group_blocks // 4,),
         in_specs=[smem, vmem, vmem],
-        out_specs=pl.BlockSpec((bs, owner_blocks * bs), lambda r: (r, 0)),
+        out_specs=pl.BlockSpec((4 * bs, owner_blocks * bs), lambda r: (r, 0)),
         scratch_shapes=[
             pltpu.SMEM((group_blocks,), jnp.int32),
             pltpu.SMEM((owners * local_scen,), jnp.int32),

time: 85.3 us -> 70.7 us (0.83)
  Pallas kernels: 77.5 us -> 66.7 us
  local copies, waits for them, and re-layouts: 7.34 us -> 3.63 us
    pallas_call x1, Pallas kernels: 67.4 us -> 61.1 us  [two_owner_form(): pl.pallas_call(functools.partial(exchange_kernel, nblk, bs), out_shape=(j...]
    unnamed x10 -> x6, local copies, waits for them, and re-layouts: 7.33 us -> 2.35 us
    pallas_call x1, Pallas kernels: 10.2 us -> 5.6 us  [two_owner_form(): pl.pallas_call(functools.partial(assemble_kernel, group_blocks, owner_blo...]
    pad x1, local copies, waits for them, and re-layouts: 0.01 us -> 1.28 us  [two_owner_form(): jnp.pad(link_ids.T, ((0, 8 - link_ids.shape[1]), (0, 128 - local_scen)))]
where the time goes in v2:
time: 70.7 us; the launch traced here: 70.3 us
  Pallas kernels  66.7 us (94%)
  local copies, waits for them, and re-layouts  3.63 us (5%)
    pallas_call x1, Pallas kernels, two_owner_form(): pl.pallas_call(functools.partial(exchange_kernel, nblk, bs), out_shape=(j...  61.1 us
    pallas_call x1, Pallas kernels, two_owner_form(): pl.pallas_call(functools.partial(assemble_kernel, group_blocks, owner_blo...  5.6 us
    unnamed x6, local copies, waits for them, and re-layouts  2.35 us

profile of v2, /device:TPU:2, one launch (start us, length us, event | category | flops | bytes accessed | tf_op | source)
XLA Modules:
  0.0 70.3 jit_solution(10347875422891984125)
XLA Ops:
  0.0 0.0 copy-start.1
  0.0 1.3 %pad.4.link_ref = s32[8,128]{1,0:T(8,128)} pad(s32[4,8]{1,0:T(4,128)} %bitcast.5, s32[]{:T(128)} %constant.0.clone.1), padding=0_4x0_120 | pad | bytes 4228 | tf_op jit(solution)/shard_map/jit(_pad)/pad | solution.py:410
  1.3 61.1 %shard_map.64 = (bf16[8,8,128,128]{3,2,1,0:T(8,128)(2,1)}, s32[8,8,128]{2,1,0:T(8,128)}) custom-call(s32[6,8,6]{2,1,0:T(8,128)} %bitcast.4, f32[8,768]{1,0:T(8,128)} %scale_ref.1, s32[8,128]{1,0:T(8,128)} %pad.4.link_ref, bf16[8,768,768]{2,1,0:T(8,128)(2,1)} %factor_ref.1, bf16[8,768,128]{2,1,0:T(8,128)(2,1)} %border_ref.1), custom_call_target="tpu_custom_call" | custom-call | tf_op jit(solution)/shard_map/pallas_call | solution.py:415
  62.4 0.0 copy-done.1
  62.4 0.0 copy-start
  62.4 1.6 %copy-done = bf16[8,8,128,128]{3,2,1,0:T(8,128)(2,1)S(1)} copy-done((bf16[8,8,128,128]{3,2,1,0:T(8,128)(2,1)S(1)}, bf16[8,8,128,128]{3,2,1,0:T(8,128)(2,1)}, u32[]{:S(2)}) %copy-start) | copy-done | bytes 2097176
  64.0 0.0 copy-start.2
  64.0 0.8 %copy-done.2 = s32[8,8,128]{2,1,0:T(8,128)S(1)} copy-done((s32[8,8,128]{2,1,0:T(8,128)S(1)}, s32[8,8,128]{2,1,0:T(8,128)}, u32[]{:S(2)}) %copy-start.2) | copy-done | bytes 32792
  64.7 5.6 %shard_map.65 = f32[2048,1024]{1,0:T(8,128)} custom-call(s32[8,8,128]{2,1,0:T(8,128)S(1)} %copy-done.2, bf16[8,8,128,128]{3,2,1,0:T(8,128)(2,1)S(1)} %copy-done, f32[64,128]{1,0:T(8,128)S(1)} %bitcast.3), custom_call_target="tpu_custom_call" | custom-call | tf_op jit(solution)/shard_map/pallas_call | solution.py:439
Async XLA Ops:
  0.0 62.4 %copy-start.1 = (f32[8192]{0:T(1024)S(1)}, f32[8192]{0:T(1024)}, u32[]{:S(2)}) copy-start(f32[8192]{0:T(1024)} %param.11) | copy-start | bytes 98308
  62.4 1.6 %copy-start = (bf16[8,8,128,128]{3,2,1,0:T(8,128)(2,1)S(1)}, bf16[8,8,128,128]{3,2,1,0:T(8,128)(2,1)}, u32[]{:S(2)}) copy-start(bf16[8,8,128,128]{3,2,1,0:T(8,128)(2,1)} %get-tuple-element.8.recv_ref) | copy-start | bytes 6291460
  64.0 0.8 %copy-start.2 = (s32[8,8,128]{2,1,0:T(8,128)S(1)}, s32[8,8,128]{2,1,0:T(8,128)}, u32[]{:S(2)}) copy-start(s32[8,8,128]{2,1,0:T(8,128)} %get-tuple-element.7.links_ref) | copy-start | bytes 98308

commit v3 on v2

--- a/solution.py
+++ b/solution.py
@@ -100,9 +100,9 @@
 def exchange_kernel(
     nblk, bs, pat_ref, scale_ref, link_ref, factor_ref, border_ref,
     recv_ref, links_ref,
-    fbuf, bbuf, own, sib, far, near_out, cross_out,
+    fbuf, bbuf, own, sib, far, near_out, cross_out, lbuf,
     f_sem, b_sem, sib_send, sib_recv, far_send, far_recv,
-    near_send, cross_send, rcv, fw_send, fw_recv, lk_send, lk_recv,
+    near_send, cross_send, both_send, rcv, fw_send, fw_recv, lk_send, lk_recv,
 ):
     scen = lax.axis_index("scen")
     tile = lax.axis_index("tile")
@@ -126,19 +126,13 @@
     barrier = pltpu.get_barrier_semaphore()
 
     def greet(k):
-        place = lax.rem(zz * 4 + tile + k + 1, 16)
+        place = lax.rem(scen * 4 + tile + k + 1, 32)
         pl.semaphore_signal(
-            barrier, inc=1, device_id=(2 * (place // 4) + yy, place % 4), device_id_type=MESH
-        )
-
-    def greet_other(k):
-        pl.semaphore_signal(
-            barrier, inc=1, device_id=(2 * k + 1 - yy, tile), device_id_type=MESH
-        )
-
-    loop(15, greet)
-    loop(4, greet_other)
-    pl.semaphore_wait(barrier, 19)
+            barrier, inc=1, device_id=(place // 4, place % 4), device_id_type=MESH
+        )
+
+    loop(31, greet)
+    pl.semaphore_wait(barrier, 31)
 
     def solve(s):
         wait_bytes(fbuf.at[s], f_sem.at[s])
@@ -221,7 +215,7 @@
                     near_out.at[half, two], recv_ref.at[scen, two], rcv.at[zz, p]
                 ).start()
 
-    def cross_copy(k, e):
+    def cross_copy(k, e, other=False):
         s = tile + 4 * k
         if e < 4:
             row = tile if e // 2 == 0 else mate
@@ -229,9 +223,12 @@
         else:
             row = 2 * xo + (e - 4) // 2
             column = tile if e % 2 == 0 else mate
+        y = 1 - yy if other else yy
+        got = (fw_recv if other else rcv).at[zz, 2 * k + tile // 2]
+        gone = both_send.at[e] if other else cross_send.at[k, e]
         return column, pltpu.make_async_remote_copy(
-            cross_out.at[k, e], recv_ref.at[scen, s], cross_send.at[k, e], rcv.at[zz, 2 * k + tile // 2],
-            device_id=(2 * column + yy, row), device_id_type=MESH,
+            cross_out.at[k, e], recv_ref.at[scen, s], gone, got,
+            device_id=(2 * column + y, row), device_id_type=MESH,
         )
 
     def cross(k):
@@ -247,6 +244,8 @@
                 cross_out[k, 4 * way + e] = out[i * bs:(i + 1) * bs, j * bs:(j + 1) * bs]
         for e in range(7, -1, -1):
             column, copy = cross_copy(k, e)
+            if k == 1:
+                cross_copy(k, e, True)[1].start()
             if e >= 2:
                 copy.start()
             else:
@@ -272,7 +271,7 @@
         if near_type:
             p = lax.rem(xo + part, 2) + 2 * (q // 4)
         else:
-            p = 2 * part + q // 4
+            p = q // 4
         src = lax.rem(zz + q, 4)
         wait_bytes(recv_ref.at[2 * src + yy, pl.ds(2 * p, 2)], rcv.at[src, p])
         forward_copy(src, p).start()
@@ -280,7 +279,7 @@
     def link_copy(k):
         other = lax.rem(scen + k + 1, 8)
         return other, pltpu.make_async_remote_copy(
-            link_ref, links_ref.at[scen], lk_send.at[k], lk_recv.at[scen],
+            lbuf, links_ref.at[scen], lk_send.at[k], lk_recv.at[scen],
             device_id=(other, tile), device_id_type=MESH,
         )
 
@@ -289,27 +288,26 @@
     loop(2, second)
     loop(2, lambda h: near(h + 2))
 
+    cross(0)
+
     @pl.when(zz // 2 == xx)
     def _():
         loop(8, functools.partial(forward, True, 0))
 
-    cross(0)
+    @pl.when(zz // 2 != xx)
+    def _():
+        loop(8, functools.partial(forward, False, 0))
+
+    cross(1)
 
     @pl.when(zz // 2 == xx)
     def _():
         loop(8, functools.partial(forward, True, 1))
 
-    @pl.when(zz // 2 != xx)
-    def _():
-        loop(8, functools.partial(forward, False, 0))
-
-    cross(1)
-    pltpu.make_async_copy(link_ref, links_ref.at[scen], lk_recv.at[scen]).start()
+    lbuf[...] = jnp.zeros_like(lbuf)
+    lbuf[:link_ref.shape[0], :link_ref.shape[1]] = link_ref[...]
+    pltpu.make_async_copy(lbuf, links_ref.at[scen], lk_recv.at[scen]).start()
     loop(7, lambda k: link_copy(k)[1].start())
-
-    @pl.when(zz // 2 != xx)
-    def _():
-        loop(8, functools.partial(forward, False, 1))
 
     loop(8, lambda s: wait_bytes(own.at[s], sib_send.at[s]))
     loop(4, lambda m: wait_bytes(own.at[m], far_send.at[m]))
@@ -334,19 +332,37 @@
                 def _():
                     copy.wait_send()
 
+    for e in range(8):
+        cross_copy(1, e, True)[1].wait_send()
     loop(7, lambda k: link_copy(k)[1].wait_send())
     loop(8, lambda p: wait_bytes(links_ref.at[p], lk_recv.at[p]))
 
-    def finish(q):
+    def forwarded(q):
+        forward_copy(q % 4, q // 4).wait_send()
+
+    def arrived(q):
+        src, p = q % 4, q // 4 + 2
+        wait_bytes(recv_ref.at[2 * src + yy, pl.ds(2 * p, 2)], rcv.at[src, p])
+
+    def arrived_other(q):
         src, p = q % 4, q // 4
-        forward_copy(src, p).wait_send()
         wait_bytes(recv_ref.at[2 * src + 1 - yy, pl.ds(2 * p, 2)], fw_recv.at[src, p])
 
-    loop(16, finish)
+    @pl.when(zz // 2 == xx)
+    def _():
+        loop(16, forwarded)
+
+    @pl.when(zz // 2 != xx)
+    def _():
+        loop(8, forwarded)
+        loop(8, arrived)
+
+    loop(16, arrived_other)
 
 
 def assemble_kernel(
-    group_blocks, owner_blocks, bs, links_ref, recv_ref, diag_ref, out_ref, head, follow, place
+    group_blocks, owner_blocks, bs, links_ref, recv_ref, diag_ref, out_ref,
+    blocks, head, follow, place, sem,
 ):
     scen = lax.axis_index("scen")
     tile = lax.axis_index("tile")
@@ -356,6 +372,8 @@
 
     @pl.when(first == 0)
     def _():
+        copy = pltpu.make_async_copy(recv_ref, blocks, sem)
+        copy.start()
         for i in range(group_blocks):
             head[i] = -1
 
@@ -374,6 +392,7 @@
             return carry
 
         lax.fori_loop(0, parts, enter, 0)
+        copy.wait()
 
     out_ref[...] = jnp.zeros_like(out_ref)
     same = lax.broadcasted_iota(jnp.int32, (bs, bs), 0) == lax.broadcasted_iota(
@@ -384,7 +403,7 @@
 
         def add(n):
             at = pl.ds(pl.multiple_of(place[n] * bs, bs), bs)
-            out_ref[rows, at] += recv_ref[n // each, n % each].astype(F32)
+            out_ref[rows, at] += blocks[n // each, n % each].astype(F32)
             return follow[n]
 
         lax.while_loop(lambda n: n >= 0, add, head[first + i])
@@ -407,7 +426,6 @@
     owners = lax.axis_size("scen")
     group_blocks = order // (tiles * bs)
     owner_blocks = order // (owners * bs)
-    links = jnp.pad(link_ids.T, ((0, 8 - link_ids.shape[1]), (0, 128 - local_scen)))
     dma = pltpu.SemaphoreType.DMA
     vmem = pl.BlockSpec(memory_space=pltpu.VMEM)
     smem = pl.BlockSpec(memory_space=pltpu.SMEM)
@@ -428,26 +446,29 @@
             pltpu.VMEM((2, 2, rows, bs), BF16),
             pltpu.VMEM((2, 8, bs, bs), BF16),
             pltpu.VMEM((2, 8, bs, bs), BF16),
+            pltpu.VMEM((8, 128), jnp.int32),
             dma((8,)), dma((8,)), dma((8,)), dma((8,)), dma((4,)), dma((2, 2)),
-            dma((2, 4)), dma((2, 8)), dma((4, 4)), dma((4, 4)), dma((4, 4)),
+            dma((2, 4)), dma((2, 8)), dma((8,)), dma((4, 4)), dma((4, 4)), dma((4, 4)),
             dma((7,)), dma((8,)),
         ],
         compiler_params=pltpu.CompilerParams(
             collective_id=0, has_side_effects=True, vmem_limit_bytes=62 * 1024 * 1024
         ),
-    )(jnp.transpose(pattern, (1, 0, 2)), row_scale, links, factor_inv, border)
+    )(jnp.transpose(pattern, (1, 0, 2)), row_scale, link_ids.T, factor_inv, border)
     return pl.pallas_call(
         functools.partial(assemble_kernel, group_blocks, owner_blocks, bs),
         out_shape=jax.ShapeDtypeStruct((group_blocks * bs, owner_blocks * bs), F32),
         grid=(group_blocks // 4,),
-        in_specs=[smem, vmem, vmem],
+        in_specs=[smem, hbm, vmem],
         out_specs=pl.BlockSpec((4 * bs, owner_blocks * bs), lambda r: (r, 0)),
         scratch_shapes=[
+            pltpu.VMEM(received.shape, BF16),
             pltpu.SMEM((group_blocks,), jnp.int32),
             pltpu.SMEM((owners * local_scen,), jnp.int32),
             pltpu.SMEM((owners * local_scen,), jnp.int32),
+            dma,
         ],
-        compiler_params=pltpu.CompilerParams(vmem_limit_bytes=24 * 1024 * 1024),
+        compiler_params=pltpu.CompilerParams(vmem_limit_bytes=62 * 1024 * 1024),
     )(all_links, received, first_diag.reshape(order // bs, bs))
 
 

time: 70.7 us -> 64.2 us (0.908)
  local copies, waits for them, and re-layouts: 3.63 us -> 0 us
  Pallas kernels: 66.7 us -> 63.8 us
    pallas_call x1, Pallas kernels: 61.1 us -> 57 us  [two_owner_form(): pl.pallas_call(functools.partial(exchange_kernel, nblk, bs), out_shape=(j...]
    unnamed x6 -> x0, local copies, waits for them, and re-layouts: 2.35 us -> none
    pad x1 -> x0, local copies, waits for them, and re-layouts: 1.28 us -> none  [two_owner_form(): jnp.pad(link_ids.T, ((0, 8 - link_ids.shape[1]), (0, 128 - local_scen)))]
    pallas_call x1, Pallas kernels: 5.6 us -> 6.89 us  [two_owner_form(): pl.pallas_call(functools.partial(assemble_kernel, group_blocks, owner_blo...]
where the time goes in v3:
time: 64.2 us; the launch traced here: 63.8 us
  Pallas kernels  63.8 us (99%)
    pallas_call x1, Pallas kernels, two_owner_form(): pl.pallas_call(functools.partial(exchange_kernel, nblk, bs), out_shape=(j...  57 us
    pallas_call x1, Pallas kernels, two_owner_form(): pl.pallas_call(functools.partial(assemble_kernel, group_blocks, owner_blo...  6.89 us

profile of v3, /device:TPU:2, one launch (start us, length us, event | category | flops | bytes accessed | tf_op | source)
XLA Modules:
  0.0 63.8 jit_solution(11734632539008682433)
XLA Ops:
  0.0 57.0 %shard_map.64 = (bf16[8,8,128,128]{3,2,1,0:T(8,128)(2,1)}, s32[8,8,128]{2,1,0:T(8,128)}) custom-call(s32[6,8,6]{2,1,0:T(8,128)} %bitcast.4, f32[8,768]{1,0:T(8,128)} %scale_ref.1, s32[4,8]{1,0:T(4,128)} %bitcast.5, bf16[8,768,768]{2,1,0:T(8,128)(2,1)} %factor_ref.1, bf16[8,768,128]{2,1,0:T(8,128)(2,1)} %border_ref.1), custom_call_target="tpu_custom_call" | custom-call | tf_op jit(solution)/shard_map/pallas_call | solution.py:433
  57.0 6.9 %shard_map.65 = f32[2048,1024]{1,0:T(8,128)} custom-call(s32[8,8,128]{2,1,0:T(8,128)} %get-tuple-element.7.links_ref, bf16[8,8,128,128]{3,2,1,0:T(8,128)(2,1)} %get-tuple-element.8.recv_ref, f32[64,128]{1,0:T(8,128)} %bitcast.3), custom_call_target="tpu_custom_call" | custom-call | tf_op jit(solution)/shard_map/pallas_call | solution.py:458
